TPU v7x, 128 devices: a whole 4x4x4 slice. The times are simulated.
128 devices in a mesh: wide: 32 (over z, y, x_hi), narrow: 4 (over x_lo, core).
Axes of the slice: x: 4 (x_hi: 2, x_lo: 2; x = x_hi * 2 + x_lo), y: 4, z: 4, core: 2. Of those that a mesh axis runs over, the one named last changes fastest.
Arguments:
- amplitudes: bfloat16 [4, 32768, 4096], P('narrow', None, 'wide'), may hold values from -6 to 6
- integrals: bfloat16 [4, 4096, 512], P('narrow'), may hold values from -0.09375 to 0.09375
- panel_order: int32 [4], replicated, may hold values from 0 to 3, each once
- row_label: int32 [4, 256], P('narrow', 'wide'), may hold values from 0 to 7
- col_label: int32 [32], replicated, may hold values from 0 to 7
- sym_map: int32 [8, 8], replicated, may hold values from 0 to 1
- row_energy: float32 [4, 32768], P('narrow', 'wide'), may hold values from 0.5 to 4
- col_energy: float32 [4, 512], replicated, may hold values from 0.5 to 4
Outputs:
- update: bfloat16 [4, 32768, 2048], P('narrow', 'wide')
Inputs may be any that keep to these rules, and one draw needn't show every extreme that they name: `panel_order`: each panel appears once.
All inputs are finite; a program needn't handle non-finite values.
Results may differ from a plain program's by a relative error of at most 0.001.
Values may be sent and summed in bfloat16 or wider, within the bound.
No kernel may reach another device: no remote copies, remote signals or barrier semaphores. Data moves between devices by JAX's collectives and lax.ppermute only.
A program may use at most 192 MiB of HBM per device.

v0:
```python
import jax
import jax.numpy as jnp
from jax import lax
from jax.sharding import PartitionSpec as P


def spread(block, axis, owner):
    block = jnp.where(lax.axis_index(axis) == owner, block, jnp.zeros_like(block))
    return lax.psum(block, axis)


def block_mask(labels_row, labels_col, sym_map):
    count = sym_map.shape[0]
    table = sym_map.astype(jnp.float32)
    left = (labels_row[:, None] == jnp.arange(count, dtype=jnp.int32)[None, :]).astype(jnp.float32)
    right = (labels_col[:, None] == jnp.arange(count, dtype=jnp.int32)[None, :]).astype(jnp.float32)
    return jnp.dot(jnp.dot(left, table), right.T)


def per_device(
    amplitudes, integrals, panel_order, row_label, col_label, sym_map, row_energy, col_energy
):
    regrouped = lax.all_to_all(amplitudes, "wide", split_axis=1, concat_axis=2, tiled=True)[0]
    rows, contr = regrouped.shape
    nbr = row_label.shape[1]
    nbc = col_label.shape[0]
    blk = rows // nbr
    mask = block_mask(row_label[0], col_label, sym_map).astype(jnp.bfloat16)
    masked = (regrouped.reshape(nbr, blk, nbc, blk) * mask[:, None, :, None]).reshape(rows, contr)
    energy_rows = row_energy[0]
    owned = integrals.shape[0]
    slots = owned * lax.axis_size("narrow")
    pieces = []
    for slot in range(slots):
        index = panel_order[slot]
        mine = lax.dynamic_index_in_dim(integrals, index % owned, 0, keepdims=False)
        panel = spread(mine, "narrow", index // owned)
        energy = lax.dynamic_index_in_dim(col_energy, index, 0, keepdims=False)
        cycle = jnp.dot(masked, panel, preferred_element_type=jnp.float32)
        pieces.append(cycle / (energy_rows[:, None] + energy[None, :]))
    return jnp.concatenate(pieces, axis=1).astype(jnp.bfloat16)[None]


def solution(mesh):
    in_specs = (
        P("narrow", None, "wide"),
        P("narrow", None, None),
        P(),
        P("narrow", "wide"),
        P(),
        P(),
        P("narrow", "wide"),
        P(),
    )
    out_specs = P("narrow", "wide", None)
    return jax.shard_map(
        per_device, mesh=mesh, in_specs=in_specs, out_specs=out_specs, check_vma=False
    )
```

profile of v0, /device:TPU:4, one launch (start us, length us, event | category | flops | bytes accessed | tf_op | source)
XLA Modules:
  0.0 507.0 jit_solution(9665287809373366172)
XLA Ops:
  6.5 0.0 all-reduce.3.cloned.1.call-start
  6.5 1.4 fusion.15
  10.4 7.7 %select_bitcast_fusion.3 = (bf16[4096,512]{1,0:T(8,128)(2,1)}, bf16[4096,512]{1,0:T(8,128)(2,1)}, bf16[4096,512]{1,0:T(8,128)(2,1)}, bf16[4096,512]{1,0:T(8,128)(2,1)}) fusion(bf16[1,4096,512]{2,1,0:T(8,128)(2,1)} %param.9, pred[]{:T(512)S(6)} %eq.52, pred[]{:T(512)S(6)} %eq.53, pred[]{:T(512)S(6)} %eq.55, pred[]{:T(512)S(6)} %eq.54), kind=kLoop, calls=%fused_computation.5 | loop fusion | flops 8388608 | bytes 20971524 | tf_op jit(solution)/shard_map/jit(_where)/select_n | solution.py:8
  18.1 0.0 all-reduce.3.cloned.1.call-update
  18.1 15.5 %copy.23 = bf16[1,32768,128]{2,0,1:T(2,128)(2,1)} copy(bf16[1,32768,128]{2,1,0:T(8,128)(2,1)} %param.8) | data formatting | bytes 16777216 | tf_op args[0]
  33.6 0.5 broadcast.32
  34.1 178.9 %reduce = bf16[32768,128]{1,0:T(8,128)(2,1)} reduce(bf16[32768,1,128]{2,1,0:T(2,128)(2,1)} %bitcast.50, bf16[]{:T(256)} %broadcast.32), dimensions={1}, to_apply=%bitcast.48.reduce_sub_computation | reduce | bytes 16777218
  213.0 20.0 %reshape.79 = bf16[32,2,65536]{2,1,0:T(2,128)(2,1)} reshape(bf16[32768,128]{1,0:T(8,128)(2,1)} %reduce) | data formatting | bytes 16777216
  233.0 0.0 copy-start.6
  233.0 0.0 copy-start.8
  233.0 0.0 copy-start.9
  233.0 0.0 copy-start.2
  233.0 11.3 %all-to-all-start = ((bf16[32,2,65536]{2,1,0:T(2,128)(2,1)}), bf16[32,2,65536]{2,1,0:T(2,128)(2,1)}, u32[]{:S(2)}, u32[]{:S(2)}) async-start(bf16[32,2,65536]{2,1,0:T(2,128)(2,1)} %reshape.79), calls=%async_computation | async-start | bytes 16777216 | tf_op jit(solution)/shard_map/all_to_all | solution.py:23
  249.2 0.0 copy-done.6
  249.2 0.0 copy-done.8
  249.2 0.0 copy-done.9
  249.3 0.3 fusion.7
  249.6 0.1 copy.17
  252.1 0.0 copy-done.2
  252.2 162.1 %all-to-all-done = bf16[32,2,65536]{2,1,0:T(2,128)(2,1)} async-done(((bf16[32,2,65536]{2,1,0:T(2,128)(2,1)}), bf16[32,2,65536]{2,1,0:T(2,128)(2,1)}, u32[]{:S(2)}, u32[]{:S(2)}) %all-to-all-start) | async-done | bytes 8388640 | tf_op jit(solution)/shard_map/all_to_all | solution.py:23
  414.3 23.4 %reshape.80 = bf16[32768,1,128]{2,1,0:T(2,128)(2,1)} reshape(bf16[32,2,65536]{2,1,0:T(2,128)(2,1)} %all-to-all-done) | data formatting | bytes 16777216
  437.6 10.6 %copy.19 = bf16[1,32768,128]{2,1,0:T(8,128)(2,1)} copy(bf16[1,32768,128]{2,0,1:T(2,128)(2,1)} %bitcast.49) | data formatting | bytes 16777216
  448.2 12.0 %copy.16 = bf16[1,1024,32,128]{1,3,2,0:T(8,128)(2,1)} copy(bf16[1,1024,32,128]{3,1,2,0:T(8,128)(2,1)} %bitcast.52) | data formatting | bytes 16777216 | tf_op jit(solution)/shard_map/all_to_all | solution.py:23
  460.2 0.0 copy-start
  460.2 1.1 mul.11
  461.3 2.2 copy-done
  463.6 0.0 copy-start.7
  463.6 4.4 bitcast_multiply_fusion
  467.9 0.0 all-reduce.3.cloned.1.call-done
  467.9 0.0 copy-done.7
  467.9 0.0 copy-start.1
  467.9 0.0 copy-start.5
  468.0 9.3 %fusion = bf16[1,1024,512]{1,2,0:T(8,128)(2,1)S(1)} fusion(bf16[1024,4096]{0,1:T(8,128)(2,1)} %bitcast_multiply_fusion, bf16[4096,512]{1,0:T(8,128)(2,1)} %get-tuple-element.5, f32[512]{0:T(512)S(1)} %bitcast.56, f32[1024]{0:T(1024)S(1)} %bitcast.57), kind=kOutput, calls=%fused_computation.10 | convolution fusion | flops 4296540160 | bytes 13637632 | tf_op jit(solution)/shard_map/dot_general | solution.py:39
  477.2 0.0 copy-done.1
  477.2 0.0 copy-done.5
  477.2 0.0 copy-start.4
  477.2 4.6 fusion.1
  481.9 0.0 copy-done.4
  481.9 0.0 copy-start.3
  481.9 4.9 fusion.2
  486.8 0.0 copy-done.3
  486.8 4.6 fusion.3
  491.4 2.3 pad_maximum_fusion
  493.7 6.4 %copy.18 = bf16[1,1024,2048]{2,1,0:T(8,128)(2,1)} copy(bf16[1,1024,2048]{1,2,0:T(8,128)(2,1)} %pad_maximum_fusion) | data formatting | bytes 8388608 | tf_op jit(solution)/shard_map/concatenate | solution.py:41
  (1 shorter events, 0.0 us)
Async XLA Ops:
  6.5 461.4 %all-reduce.3.cloned.1.call-start = ((), (), s32[]{:S(2)}) async-start(), calls=%async_computation.1 | async-start | bytes 33554432 | tf_op jit(solution)/shard_map/psum | solution.py:9
  233.0 16.3 %copy-start.6 = (s32[8,8]{1,0:T(8,128)S(1)}, s32[8,8]{1,0:T(8,128)}, u32[]{:S(2)}) copy-start(s32[8,8]{1,0:T(8,128)} %param.13) | copy-start | bytes 772
  233.0 16.3 %copy-start.8 = (s32[32]{0:T(128)S(1)}, s32[32]{0:T(128)}, u32[]{:S(2)}) copy-start(s32[32]{0:T(128)} %param.12) | copy-start | bytes 388
  233.0 16.3 %copy-start.9 = (s32[1,8]{1,0:T(1,128)S(1)}, s32[1,8]{1,0:T(1,128)}, u32[]{:S(2)}) copy-start(s32[1,8]{1,0:T(1,128)} %param.11) | copy-start | bytes 100
  233.0 19.2 %copy-start.2 = (f32[4,512]{1,0:T(4,128)S(1)}, f32[4,512]{1,0:T(4,128)}, u32[]{:S(2)}) copy-start(f32[4,512]{1,0:T(4,128)} %param.15) | copy-start | bytes 24580
  233.0 181.3 %all-to-all-start = ((bf16[32,2,65536]{2,1,0:T(2,128)(2,1)}), bf16[32,2,65536]{2,1,0:T(2,128)(2,1)}, u32[]{:S(2)}, u32[]{:S(2)}) async-start(bf16[32,2,65536]{2,1,0:T(2,128)(2,1)} %reshape.79), calls=%async_computation | async-start | bytes 16777216 | tf_op jit(solution)/shard_map/all_to_all | solution.py:23
  460.2 3.4 copy-start
  463.6 4.4 copy-start.7
  467.9 9.3 %copy-start.1 = (bf16[1024,4096]{0,1:T(8,128)(2,1)S(1)}, bf16[1024,4096]{0,1:T(8,128)(2,1)}, u32[]{:S(2)}) copy-start(bf16[1024,4096]{0,1:T(8,128)(2,1)} %bitcast_multiply_fusion) | copy-start | bytes 25165828
  467.9 9.3 %copy-start.5 = (bf16[4096,512]{1,0:T(8,128)(2,1)S(1)}, bf16[4096,512]{1,0:T(8,128)(2,1)}, u32[]{:S(2)}) copy-start(bf16[4096,512]{1,0:T(8,128)(2,1)} %get-tuple-element.6) | copy-start | bytes 12582916
  477.2 4.7 copy-start.4
  481.9 4.9 copy-start.3
Sparse Core Ops, SparseCore 0:
  18.2 367.3 all-reduce.2
where the time goes:
time: 509 us; the launch traced here: 507 us
  other arithmetic  193 us (38%)
  waiting for transfers between devices  162 us (32%)
  local copies, waits for them, and re-layouts  93.2 us (18%)
  matrix products  23.7 us (5%)
  between operations  23.5 us (5%)
  starting transfers between devices  11.3 us (2%)
    unnamed x1, other arithmetic  179 us
    all_to_all x1, waiting for transfers between devices, per_device(): lax.all_to_all(amplitudes, 'wide', split_axis=1, concat_axis=2, tiled=True)  162 us
    unnamed x25, local copies, waits for them, and re-layouts  72.2 us
    dot_general x4, matrix products, per_device(): cycle = jnp.dot(masked, panel, preferred_element_type=jnp.float32)  23.4 us
    all_to_all x1, local copies, waits for them, and re-layouts, per_device(): lax.all_to_all(amplitudes, 'wide', split_axis=1, concat_axis=2, tiled=True)  12 us
    all_to_all x1, starting transfers between devices, per_device(): lax.all_to_all(amplitudes, 'wide', split_axis=1, concat_axis=2, tiled=True)  11.3 us
  transfers between devices with their start and end apart: 2, of which 1 were waited for; matrix products, arithmetic and copies ran while one was open for 53% of the time, Pallas kernels for 0%

commit v1 on v0

v1 whole, which is shorter than its diff:
```python
import functools
import jax
import jax.numpy as jnp
from jax import lax
from jax.experimental import pallas as pl
from jax.experimental.pallas import tpu as pltpu
from jax.sharding import PartitionSpec as P

AXES = ("wide", "narrow")
CHUNKS = (512, 512)


def x_of(device):
    return device // 4 % 2 * 2 + device // 2 % 2


def shift_x(devices, step):
    pairs = []
    for i in range(devices):
        x = (x_of(i) + step) % 4
        pairs.append((i, i // 8 * 8 + x // 2 * 4 + x % 2 * 2 + i % 2))
    return pairs


def swap_core(devices):
    return [(i, i ^ 1) for i in range(devices)]


def cycle_kernel(
    held_ref, slot_ref, row_label_ref, col_label_ref, sym_ref,
    amp_ref, row_energy_ref, col_energy_ref, *refs, first, blk, pieces
):
    panel_refs = refs[: sum(pieces)]
    refs = refs[sum(pieces):]
    if len(refs) == 5:
        refs = refs[1:]
    out_ref, masked, panel, sems = refs
    step = pl.program_id(0)
    nbc = amp_ref.shape[0]
    rows = amp_ref.shape[1]
    depth = panel.shape[1]

    def copies(k):
        at = sum(pieces[:k])
        size = depth // pieces[k]
        return [
            pltpu.make_async_copy(
                panel_refs[at + i], panel.at[k, pl.ds(i * size, size)], sems.at[at + i]
            )
            for i in range(pieces[k])
        ]

    @pl.when(step == 0)
    def _():
        for k in range(len(pieces)):
            for copy in copies(k):
                copy.start()
        for i in range(rows // blk):
            for c in range(nbc):
                keep = sym_ref[row_label_ref[first + i], col_label_ref[c]]
                tile = amp_ref[c, i * blk:(i + 1) * blk, :]
                masked[i * blk:(i + 1) * blk, c * blk:(c + 1) * blk] = tile * keep.astype(
                    jnp.float32
                ).astype(tile.dtype)

    for k in range(len(pieces)):

        @pl.when(step == k)
        def _():
            for copy in copies(k):
                copy.wait()

    cycle = jnp.dot(masked[...], panel[step], preferred_element_type=jnp.float32)
    energy = row_energy_ref[...] + col_energy_ref[pl.ds(held_ref[step], 1), :]
    out_ref[...] = (cycle / energy).astype(out_ref.dtype)


def update_rows(amp, panels, before, start, total, scalars, row_energy, col_energy, blk):
    nbc, rows, _ = amp.shape
    pieces = tuple(len(p) for p in panels)
    flat = [piece for p in panels for piece in p]
    depth = sum(p.shape[0] for p in panels[0])
    qp = flat[0].shape[1]
    at = start // rows
    slots = len(panels)
    whole = pl.BlockSpec(memory_space=pl.ANY)
    in_specs = [
        pl.BlockSpec((nbc, rows, blk), lambda k, *_: (0, 0, 0)),
        pl.BlockSpec((rows, 1), lambda k, *_: (at, 0)),
        pl.BlockSpec(col_energy.shape, lambda k, *_: (0, 0)),
    ] + [whole] * len(flat)
    args = [amp, row_energy, col_energy] + flat
    aliases = {}
    if before is not None:
        in_specs.append(whole)
        args.append(before)
        aliases = {len(scalars) + len(args) - 1: 0}
    return pl.pallas_call(
        functools.partial(cycle_kernel, first=start // blk, blk=blk, pieces=pieces),
        grid_spec=pltpu.PrefetchScalarGridSpec(
            num_scalar_prefetch=len(scalars),
            grid=(slots,),
            in_specs=in_specs,
            out_specs=pl.BlockSpec((rows, qp), lambda k, held, slot, *_: (at, slot[k])),
            scratch_shapes=[
                pltpu.VMEM((rows, depth), amp.dtype),
                pltpu.VMEM((slots, depth, qp), amp.dtype),
                pltpu.SemaphoreType.DMA((len(flat),)),
            ],
        ),
        out_shape=jax.ShapeDtypeStruct((total, slots * qp), jnp.bfloat16),
        input_output_aliases=aliases,
        compiler_params=pltpu.CompilerParams(vmem_limit_bytes=44 * 2**20),
        cost_estimate=pl.CostEstimate(
            flops=2 * rows * depth * qp * slots,
            bytes_accessed=2 * (rows * depth + slots * depth * qp + rows * slots * qp),
            transcendentals=0,
        ),
    )(*scalars, *args)


def per_device(
    amplitudes, integrals, panel_order, row_label, col_label, sym_map, row_energy, col_energy
):
    wide, narrow = lax.axis_size("wide"), lax.axis_size("narrow")
    devices = wide * narrow
    send = functools.partial(lax.ppermute, axis_name=AXES)
    own = integrals[0]
    half = own.shape[0] // 2
    far = [
        send(own[:half], perm=shift_x(devices, 1)),
        send(own[half:], perm=shift_x(devices, -1)),
    ]
    twin = send(own, perm=swap_core(devices))
    far_twin = [send(piece, perm=swap_core(devices)) for piece in far]
    panels = [[own], [twin], far, far_twin]
    me = lax.axis_index("narrow")
    held = jnp.stack([me, me ^ 1, me ^ 2, me ^ 3]).astype(jnp.int32)
    slot = jnp.sum(
        jnp.where(
            held[:, None] == panel_order[None, :],
            jnp.arange(narrow, dtype=jnp.int32)[None, :],
            0,
        ),
        axis=1,
    ).astype(jnp.int32)
    total = amplitudes.shape[1] // wide
    blk = amplitudes.shape[2]
    by_target = amplitudes[0].reshape(wide, total, blk)
    scalars = (held, slot, row_label[0], col_label, sym_map)
    column = row_energy.reshape(total, 1)
    out = None
    start = 0
    for rows in CHUNKS:
        amp = lax.all_to_all(by_target[:, start:start + rows], "wide", split_axis=0, concat_axis=0)
        out = update_rows(
            amp, panels, out, start, total, scalars, column, col_energy, blk
        )
        start += rows
    return out[None]


def solution(mesh):
    in_specs = (
        P("narrow", None, "wide"),
        P("narrow", None, None),
        P(),
        P("narrow", "wide"),
        P(),
        P(),
        P("narrow", "wide"),
        P(),
    )
    out_specs = P("narrow", "wide", None)
    return jax.shard_map(
        per_device, mesh=mesh, in_specs=in_specs, out_specs=out_specs, check_vma=False
    )
```

time: 509 us -> 179 us (0.35)
  other arithmetic: 193 us -> 0.26 us
  local copies, waits for them, and re-layouts: 93.2 us -> 10.8 us
  waiting for transfers between devices: 162 us -> 111 us
  Pallas kernels: 0 us -> 30.8 us
  matrix products: 23.7 us -> 0 us
  between operations: 23.5 us -> 0.08 us
  starting transfers between devices: 11.3 us -> 24 us
    unnamed x1 -> x0, other arithmetic: 179 us -> none
    all_to_all x1 -> x2, waiting for transfers between devices: 162 us -> 76.7 us  [per_device(): lax.all_to_all(by_target[:, start:start + rows], 'wide', split_axis=0, co...]
    unnamed x25 -> x12, local copies, waits for them, and re-layouts: 72.2 us -> 0.03 us
    ppermute x0 -> x5, waiting for transfers between devices: none -> 34.6 us  [the longest x1 28.1 us: per_device(): send(own[half:], perm=shift_x(devices, -1))]
    pallas_call x0 -> x2, Pallas kernels: none -> 30.8 us  [update_rows(): pl.pallas_call(functools.partial(cycle_kernel, first=start // blk, blk=bl...]
    dot_general x5 -> x0, matrix products: 23.7 us -> none  [the longest x4 23.4 us: per_device(): cycle = jnp.dot(masked, panel, preferred_element_type=jnp.float32)]
    all_to_all x1 -> x0, local copies, waits for them, and re-layouts: 12 us -> none  [per_device(): lax.all_to_all(amplitudes, 'wide', split_axis=1, concat_axis=2, tiled=True)]
    all_to_all x1 -> x2, starting transfers between devices: 11.3 us -> 21.5 us  [per_device(): lax.all_to_all(by_target[:, start:start + rows], 'wide', split_axis=0, co...]
  transfers between devices with their start and end apart: 2 -> 7, of which waited for: 1 -> 5; matrix products, arithmetic and copies ran while one was open for 53% -> 3% of each run, Pallas kernels for 0% -> 9%
where the time goes in v1:
time: 179 us; the launch traced here: 177 us
  waiting for transfers between devices  111 us (62%)
  Pallas kernels  30.8 us (17%)
  starting transfers between devices  24 us (13%)
  local copies, waits for them, and re-layouts  10.8 us (6%)
    all_to_all x2, waiting for transfers between devices, per_device(): lax.all_to_all(by_target[:, start:start + rows], 'wide', split_axis=0, co...  76.7 us
    pallas_call x2, Pallas kernels, update_rows(): pl.pallas_call(functools.partial(cycle_kernel, first=start // blk, blk=bl...  30.8 us
    ppermute x1, waiting for transfers between devices, per_device(): send(own[half:], perm=shift_x(devices, -1))  28.1 us
    all_to_all x2, starting transfers between devices, per_device(): lax.all_to_all(by_target[:, start:start + rows], 'wide', split_axis=0, co...  21.5 us
    ppermute x2, waiting for transfers between devices, per_device(): far_twin = [send(piece, perm=swap_core(devices)) for piece in far]  6.49 us
    slice x1, local copies, waits for them, and re-layouts, per_device(): by_target[:, start:start + rows]  6.01 us
    slice x1, local copies, waits for them, and re-layouts, per_device(): own[half:]  4.51 us
  transfers between devices with their start and end apart: 7, of which 5 were waited for; matrix products, arithmetic and copies ran while one was open for 3% of the time, Pallas kernels for 9%

profile of v1, /device:TPU:4, one launch (start us, length us, event | category | flops | bytes accessed | tf_op | source)
XLA Modules:
  0.0 177.2 jit_solution(12784115977650296779)
XLA Ops:
  0.0 6.0 %fusion = (bf16[32,512,128]{2,1,0:T(8,128)(2,1)}, bf16[32,512,128]{2,1,0:T(8,128)(2,1)}) fusion(bf16[32,1024,128]{2,1,0:T(8,128)(2,1)} %bitcast.15), kind=kLoop, calls=%fused_computation.4 | loop fusion | bytes 16777216 | tf_op jit(solution)/shard_map/slice | solution.py:155
  6.0 11.1 %all-to-all-start.1 = ((bf16[32,512,128]{2,1,0:T(8,128)(2,1)}), bf16[32,512,128]{2,1,0:T(8,128)(2,1)}, u32[]{:S(2)}, u32[]{:S(2)}) async-start(bf16[32,512,128]{2,1,0:T(8,128)(2,1)} %get-tuple-element.5), calls=%async_computation.1 | async-start | bytes 8388608 | tf_op jit(solution)/shard_map/all_to_all | solution.py:155
  17.1 4.5 %slice_bitcast_fusion = (bf16[2048,512]{1,0:T(8,128)(2,1)}, bf16[2048,512]{1,0:T(8,128)(2,1)}) fusion(bf16[1,4096,512]{2,1,0:T(8,128)(2,1)} %param.9), kind=kLoop, calls=%fused_computation | loop fusion | bytes 8388608 | tf_op jit(solution)/shard_map/slice | solution.py:132
  21.6 0.0 collective-permute-start.2
  21.7 2.0 %collective-permute-start.1 = (bf16[2048,512]{1,0:T(8,128)(2,1)}, bf16[2048,512]{1,0:T(8,128)(2,1)}, u32[]{:S(2)}, u32[]{:S(2)}) collective-permute-start(bf16[2048,512]{1,0:T(8,128)(2,1)} %get-tuple-element.8), channel_id=1, source_target_pairs={{0,2},{1,3},{2,4},{3,5},{4,6},{5,7},{6,0},{7,1},{8,10},{9,11},{10,... | collective-permute-start | bytes 6291464 | tf_op jit(solution)/shard_map/ppermute | solution.py:131
  23.7 0.0 collective-permute-start
  23.7 48.9 %all-to-all-done.1.amp_ref = bf16[32,512,128]{2,1,0:T(8,128)(2,1)} async-done(((bf16[32,512,128]{2,1,0:T(8,128)(2,1)}), bf16[32,512,128]{2,1,0:T(8,128)(2,1)}, u32[]{:S(2)}, u32[]{:S(2)}) %all-to-all-start.1) | async-done | bytes 4194336 | tf_op jit(solution)/shard_map/all_to_all | solution.py:155
  72.5 0.0 copy-start.4
  72.5 0.0 copy-start.5
  72.6 0.0 copy-start
  72.6 0.0 copy-start.1
  72.6 0.0 copy-start.2
  72.6 0.0 copy-start.3
  72.6 10.3 %all-to-all-start = ((bf16[32,512,128]{2,1,0:T(8,128)(2,1)}), bf16[32,512,128]{2,1,0:T(8,128)(2,1)}, u32[]{:S(2)}, u32[]{:S(2)}) async-start(bf16[32,512,128]{2,1,0:T(8,128)(2,1)} %get-tuple-element.6), calls=%async_computation | async-start | bytes 8388608 | tf_op jit(solution)/shard_map/all_to_all | solution.py:155
  82.9 28.1 %collective-permute-done.2.refs_3_ = bf16[2048,512]{1,0:T(8,128)(2,1)S(1)} collective-permute-done((bf16[2048,512]{1,0:T(8,128)(2,1)}, bf16[2048,512]{1,0:T(8,128)(2,1)S(1)}, u32[]{:S(2)}, u32[]{:S(2)}) %collective-permute-start.2) | collective-permute-done | bytes 2097184 | tf_op jit(solution)/shard_map/ppermute | solution.py:132
  111.0 0.0 collective-permute-start.4
  111.0 0.0 collective-permute-done.1.refs_2_
  111.0 0.5 collective-permute-start.3
  111.5 0.0 copy-done.4
  111.5 0.2 copy.13.row_energy_ref
  111.8 0.1 pad_add_fusion.held_ref
  111.9 0.0 copy-done.5
  111.9 0.2 select_reduce_fusion.slot_ref
  112.0 6.2 %collective-permute-done.4.refs_5_ = bf16[2048,512]{1,0:T(8,128)(2,1)} collective-permute-done((bf16[2048,512]{1,0:T(8,128)(2,1)S(1)}, bf16[2048,512]{1,0:T(8,128)(2,1)}, u32[]{:S(2)}, u32[]{:S(2)}) %collective-permute-start.4) | collective-permute-done | bytes 2097184 | tf_op jit(solution)/shard_map/ppermute | solution.py:135
  118.2 0.3 collective-permute-done.3.refs_4_
  118.5 0.0 collective-permute-done.refs_1_
  118.5 0.0 copy-done
  118.5 0.0 copy-done.1
  118.5 0.0 copy-done.2
  118.5 0.0 copy-done.3
  118.6 15.4 %shard_map.82.refs_6_ = bf16[1024,2048]{1,0:T(8,128)(2,1)} custom-call(s32[4]{0:T(128)S(1)} %pad_add_fusion.held_ref, s32[4]{0:T(128)S(1)} %select_reduce_fusion.slot_ref, s32[8]{0:T(128)S(1)} %bitcast.13, s32[32]{0:T(128)S(1)} %copy-done.3, s32[8,8]{1,0:T(8,128)S(1)} %copy-done.1, bf16[32,512,128]{2,1,0:T(8,128)(2,1)} %all-to-all-done.1.amp_ref, ...), custom_call_target="tpu_custom_call" | custom-call | flops 8589934592 | bytes 23068672 | tf_op jit(solution)/shard_map/pallas_call | solution.py:98
  134.0 27.8 %all-to-all-done.amp_ref = bf16[32,512,128]{2,1,0:T(8,128)(2,1)} async-done(((bf16[32,512,128]{2,1,0:T(8,128)(2,1)}), bf16[32,512,128]{2,1,0:T(8,128)(2,1)}, u32[]{:S(2)}, u32[]{:S(2)}) %all-to-all-start) | async-done | bytes 4194336 | tf_op jit(solution)/shard_map/all_to_all | solution.py:155
  161.8 15.4 %shard_map.83 = bf16[1024,2048]{1,0:T(8,128)(2,1)} custom-call(s32[4]{0:T(128)S(1)} %pad_add_fusion.held_ref, s32[4]{0:T(128)S(1)} %select_reduce_fusion.slot_ref, s32[8]{0:T(128)S(1)} %bitcast.14, s32[32]{0:T(128)S(1)} %copy-done.3, s32[8,8]{1,0:T(8,128)S(1)} %copy-done.1, ...), custom_call_target="tpu_custom_call", output_to_operand_aliasing={{}: (14, {})} | custom-call | flops 8589934592 | bytes 23068672 | tf_op jit(solution)/shard_map/pallas_call | solution.py:98
Async XLA Ops:
  6.0 66.5 %all-to-all-start.1 = ((bf16[32,512,128]{2,1,0:T(8,128)(2,1)}), bf16[32,512,128]{2,1,0:T(8,128)(2,1)}, u32[]{:S(2)}, u32[]{:S(2)}) async-start(bf16[32,512,128]{2,1,0:T(8,128)(2,1)} %get-tuple-element.5), calls=%async_computation.1 | async-start | bytes 8388608 | tf_op jit(solution)/shard_map/all_to_all | solution.py:155
  21.6 89.4 %collective-permute-start.2 = (bf16[2048,512]{1,0:T(8,128)(2,1)}, bf16[2048,512]{1,0:T(8,128)(2,1)S(1)}, u32[]{:S(2)}, u32[]{:S(2)}) collective-permute-start(bf16[2048,512]{1,0:T(8,128)(2,1)} %get-tuple-element.7), channel_id=1, source_target_pairs={{0,6},{1,7},{2,0},{3,1},{4,2},{5,3},{6,4},{7,5},{8,14},{9,15},{10,... | collective-permute-start | bytes 6291464 | tf_op jit(solution)/shard_map/ppermute | solution.py:132
  21.7 89.4 %collective-permute-start.1 = (bf16[2048,512]{1,0:T(8,128)(2,1)}, bf16[2048,512]{1,0:T(8,128)(2,1)}, u32[]{:S(2)}, u32[]{:S(2)}) collective-permute-start(bf16[2048,512]{1,0:T(8,128)(2,1)} %get-tuple-element.8), channel_id=1, source_target_pairs={{0,2},{1,3},{2,4},{3,5},{4,6},{5,7},{6,0},{7,1},{8,10},{9,11},{10,... | collective-permute-start | bytes 6291464 | tf_op jit(solution)/shard_map/ppermute | solution.py:131
  23.7 94.9 %collective-permute-start = (bf16[4096,512]{1,0:T(8,128)(2,1)}, bf16[4096,512]{1,0:T(8,128)(2,1)}, u32[]{:S(2)}, u32[]{:S(2)}) collective-permute-start(bf16[4096,512]{1,0:T(8,128)(2,1)} %bitcast.7.refs_0_), channel_id=1, source_target_pairs={{0,1},{1,0},{2,3},{3,2},{4,5},{5,4},{6,7},{7,6},{8,9},{9,8},{10,11... | collective-permute-start | bytes 12582920 | tf_op jit(solution)/shard_map/ppermute | solution.py:134
  72.5 39.0 %copy-start.4 = (f32[1,1024]{1,0:T(1,128)S(1)}, f32[1,1024]{1,0:T(1,128)}, u32[]{:S(2)}) copy-start(f32[1,1024]{1,0:T(1,128)} %param.14) | copy-start | bytes 12292
  72.5 39.3 %copy-start.5 = (s32[4]{0:T(128)S(1)}, s32[4]{0:T(128)}, u32[]{:S(2)}) copy-start(s32[4]{0:T(128)} %param.10) | copy-start | bytes 52
  72.6 46.0 %copy-start = (f32[4,512]{1,0:T(4,128)S(1)}, f32[4,512]{1,0:T(4,128)}, u32[]{:S(2)}) copy-start(f32[4,512]{1,0:T(4,128)} %col_energy_ref.3) | copy-start | bytes 24580
  72.6 46.0 %copy-start.1 = (s32[8,8]{1,0:T(8,128)S(1)}, s32[8,8]{1,0:T(8,128)}, u32[]{:S(2)}) copy-start(s32[8,8]{1,0:T(8,128)} %sym_ref.3) | copy-start | bytes 772
  72.6 46.0 %copy-start.2 = (s32[1,8]{1,0:T(1,128)S(1)}, s32[1,8]{1,0:T(1,128)}, u32[]{:S(2)}) copy-start(s32[1,8]{1,0:T(1,128)} %param.11) | copy-start | bytes 100
  72.6 46.0 %copy-start.3 = (s32[32]{0:T(128)S(1)}, s32[32]{0:T(128)}, u32[]{:S(2)}) copy-start(s32[32]{0:T(128)} %col_label_ref.3) | copy-start | bytes 388
  72.6 89.2 %all-to-all-start = ((bf16[32,512,128]{2,1,0:T(8,128)(2,1)}), bf16[32,512,128]{2,1,0:T(8,128)(2,1)}, u32[]{:S(2)}, u32[]{:S(2)}) async-start(bf16[32,512,128]{2,1,0:T(8,128)(2,1)} %get-tuple-element.6), calls=%async_computation | async-start | bytes 8388608 | tf_op jit(solution)/shard_map/all_to_all | solution.py:155
  111.0 7.2 %collective-permute-start.4 = (bf16[2048,512]{1,0:T(8,128)(2,1)S(1)}, bf16[2048,512]{1,0:T(8,128)(2,1)}, u32[]{:S(2)}, u32[]{:S(2)}) collective-permute-start(bf16[2048,512]{1,0:T(8,128)(2,1)S(1)} %collective-permute-done.2.refs_3_), channel_id=1, source_target_pairs={{0,1},{1,0},{2,3},{3,2},{4,5},{5,4},{6,7},{7,6},{8,9},{9,8},{10,11... | collective-permute-start | bytes 6291464 | tf_op jit(solution)/shard_map/ppermute | solution.py:135
  111.0 7.5 %collective-permute-start.3 = (bf16[2048,512]{1,0:T(8,128)(2,1)}, bf16[2048,512]{1,0:T(8,128)(2,1)}, u32[]{:S(2)}, u32[]{:S(2)}) collective-permute-start(bf16[2048,512]{1,0:T(8,128)(2,1)} %collective-permute-done.1.refs_2_), channel_id=1, source_target_pairs={{0,1},{1,0},{2,3},{3,2},{4,5},{5,4},{6,7},{7,6},{8,9},{9,8},{10,11... | collective-permute-start | bytes 6291464 | tf_op jit(solution)/shard_map/ppermute | solution.py:135

commit v2 on v0

v2 whole, which is shorter than its diff:
```python
import functools
import jax
import jax.numpy as jnp
from jax import lax
from jax.experimental import pallas as pl
from jax.experimental.pallas import tpu as pltpu
from jax.sharding import PartitionSpec as P

AXES = ("wide", "narrow")
CHUNKS = (640, 384)
ANY = pl.BlockSpec(memory_space=pl.ANY)
VMEM = pl.BlockSpec(memory_space=pltpu.VMEM)
HBM = pl.BlockSpec(memory_space=pltpu.HBM)
SMEM = pl.BlockSpec(memory_space=pltpu.SMEM)


def place(i):
    return i // 32, i // 8 % 4, i // 4 % 2 * 2 + i // 2 % 2, i % 2


def shift(devices, dz=0, dy=0, dx=0, dc=0):
    pairs = []
    for i in range(devices):
        z, y, x, c = place(i)
        z, y, x, c = (z + dz) % 4, (y + dy) % 4, (x + dx) % 4, (c + dc) % 2
        pairs.append((i, z * 32 + y * 8 + x // 2 * 4 + x % 2 * 2 + c))
    return pairs


def after(value, *others):
    return lax.optimization_barrier((value, *others))[0]


def cycle_kernel(
    scalar_ref, amp_ref, row_energy_ref, col_energy_ref, *refs, start, slots, labels, cuts
):
    *refs, masked, staged, panels, store_sems, load_sems, keep_sems = refs
    out_ref = refs[-2] if cuts else refs[-1]
    kept = refs[-1] if cuts else refs[0]
    count = max((which for which, _, _ in cuts), default=-1) + 1
    nbc, rows, blk = amp_ref.shape
    qp = staged.shape[2]
    held, slot, row_label = 0, slots, 2 * slots
    col_label = row_label + labels[0]
    table = col_label + nbc
    offset = table + labels[1] * labels[1]

    def loads(k):
        if not cuts:
            return [pltpu.make_async_copy(kept.at[k], panels.at[k], load_sems.at[k])]
        if k < 2:
            return [pltpu.make_async_copy(refs[k], panels.at[k], load_sems.at[k])]
        out = []
        for n, (which, at, size) in enumerate(cuts):
            to = pl.multiple_of(scalar_ref[offset + n], 128)
            out.append(
                pltpu.make_async_copy(
                    refs[2 + (k - 2) * count + which].at[pl.ds(at, size)],
                    panels.at[k, pl.ds(to, size)],
                    load_sems.at[k],
                )
            )
        return out

    def mask_column(c, carry):
        for i in range(rows // blk):
            row = scalar_ref[row_label + start // blk + i]
            kept_block = scalar_ref[table + row * labels[1] + scalar_ref[col_label + c]]
            tile = amp_ref[c, i * blk:(i + 1) * blk, :]
            at = pl.multiple_of(c * blk, blk)
            masked[i * blk:(i + 1) * blk, pl.ds(at, blk)] = tile * kept_block.astype(
                jnp.float32
            ).astype(tile.dtype)
        return carry

    def store(k):
        at = pl.multiple_of(scalar_ref[slot + k] * qp, qp)
        return pltpu.make_async_copy(
            staged.at[k], out_ref.at[pl.ds(start, rows), pl.ds(at, qp)], store_sems.at[k]
        )

    def keep(k):
        return pltpu.make_async_copy(panels.at[k], kept.at[k], keep_sems.at[k])

    for copy in loads(0):
        copy.start()
    lax.fori_loop(0, nbc, mask_column, 0)
    for copy in loads(1):
        copy.start()
    for k in range(slots):
        for copy in loads(k):
            copy.wait()
        if k + 2 < slots:
            for copy in loads(k + 2):
                copy.start()
        if cuts:
            keep(k).start()
        cycle = jnp.dot(masked[...], panels[k], preferred_element_type=jnp.float32)
        energy = row_energy_ref[...] + col_energy_ref[pl.ds(scalar_ref[held + k], 1), :]
        staged[k] = (cycle / energy).astype(staged.dtype)
        store(k).start()
    for k in range(slots):
        store(k).wait()
        if cuts:
            keep(k).wait()


def update_rows(amp, panels, cuts, before, start, total, scalars, labels, row_energy, col_energy):
    nbc, rows, blk = amp.shape
    depth, qp = nbc * blk, panels[0].shape[-1]
    slots = 4
    args = [scalars, amp, row_energy[start:start + rows], col_energy] + panels
    specs = [SMEM] + [VMEM] * 3
    out_shape = [jax.ShapeDtypeStruct((total, slots * qp), jnp.bfloat16)]
    aliases = {}
    if before is None:
        specs += [HBM] * len(panels)
        out_shape.append(jax.ShapeDtypeStruct((slots, depth, qp), amp.dtype))
    else:
        specs += [HBM, ANY]
        aliases = {len(args): 0}
        args.append(before)
        cuts = ()
    return pl.pallas_call(
        functools.partial(cycle_kernel, start=start, slots=slots, labels=labels, cuts=cuts),
        in_specs=specs,
        out_specs=[ANY, HBM][: len(out_shape)],
        scratch_shapes=[
            pltpu.VMEM((rows, depth), amp.dtype),
            pltpu.VMEM((slots, rows, qp), jnp.bfloat16),
            pltpu.VMEM((slots, depth, qp), amp.dtype),
            pltpu.SemaphoreType.DMA((slots,)),
            pltpu.SemaphoreType.DMA((slots,)),
            pltpu.SemaphoreType.DMA((slots,)),
        ],
        out_shape=out_shape,
        input_output_aliases=aliases,
        compiler_params=pltpu.CompilerParams(vmem_limit_bytes=(54 if before is None else 50) * 2**20),
        cost_estimate=pl.CostEstimate(
            flops=2 * rows * depth * qp * slots,
            bytes_accessed=2 * (rows * depth + slots * depth * qp + rows * slots * qp),
            transcendentals=0,
        ),
    )(*args)


def per_device(
    amplitudes, integrals, panel_order, row_label, col_label, sym_map, row_energy, col_energy
):
    wide, narrow = lax.axis_size("wide"), lax.axis_size("narrow")
    total = amplitudes.shape[1] // wide
    blk = amplitudes.shape[2]
    by_target = amplitudes[0].reshape(wide, total, blk)

    def send(value, **way):
        return lax.ppermute(value, AXES, shift(wide * narrow, **way))

    own = integrals[0]
    depth = own.shape[0]
    half, part, bit = depth // 2, depth // 8, depth // 16
    w = lax.axis_index("wide")
    z, y = w // 8, w // 2 % 4

    def a_at(step):
        return (z + 2 * y + 4 + step) % 4 * part

    def b_at(step):
        return half + (2 * z + y + 4 + step) % 4 * part

    a = send(lax.dynamic_slice_in_dim(own, a_at(0), part, 0), dx=1)
    b = send(lax.dynamic_slice_in_dim(own, b_at(0), part, 0), dx=-1)
    twin = send(own, dc=1)
    amps, start = [], 0
    for rows in CHUNKS:
        block = by_target[:, start:start + rows]
        gate = amps[-1:] if amps else [a, b, twin]
        block = after(block, *gate)
        amps.append(lax.all_to_all(block, "wide", split_axis=0, concat_axis=0))
        start += rows
    z_down = send(jnp.concatenate([a, b[:bit]]), dz=1)
    z_up = send(jnp.concatenate([a, b[bit:]]), dz=-1)
    y_down = send(jnp.concatenate([b, a[:bit]]), dy=1)
    y_up = send(jnp.concatenate([b, a[bit:]]), dy=-1)
    pieces = [a, b, z_down, z_up, y_down, y_up]
    cuts = [(0, 0, part), (1, 0, part)]
    for n in range(2, 6):
        cuts += [(n, 0, part), (n, part, bit)]
    offsets = [
        a_at(0), b_at(0),
        a_at(-1), b_at(2), a_at(1), b_at(2) + bit,
        b_at(-1), a_at(2), b_at(1), a_at(2) + bit,
    ]
    za, zb, ya, yb = pieces[2:]
    za, zb = lax.optimization_barrier((za, zb, ya, yb))[:2]
    za, zb = send(za, dc=1), send(zb, dc=1)
    ya, yb = lax.optimization_barrier((ya, yb, za, zb))[:2]
    twins = [send(a, dc=1), send(b, dc=1), za, zb, send(ya, dc=1), send(yb, dc=1)]
    panels = [own, twin] + pieces + twins
    me = lax.axis_index("narrow")
    held = jnp.stack([me, me ^ 1, me ^ 2, me ^ 3]).astype(jnp.int32)
    slot = jnp.sum(
        jnp.where(
            held[:, None] == panel_order[None, :],
            jnp.arange(narrow, dtype=jnp.int32)[None, :],
            0,
        ),
        axis=1,
    ).astype(jnp.int32)
    scalars = jnp.concatenate([held, slot, row_label[0], col_label, sym_map.reshape(-1), jnp.stack(offsets)])
    scalars = scalars.astype(jnp.int32)
    labels = (row_label.shape[1], sym_map.shape[1])
    column = row_energy.reshape(total, 1)
    out = None
    start = 0
    for rows, amp in zip(CHUNKS, amps):
        out, *kept = update_rows(
            amp, panels, tuple(cuts), out, start, total, scalars, labels, column, col_energy
        )
        panels = kept or panels
        start += rows
    return out[None]


def solution(mesh):
    in_specs = (
        P("narrow", None, "wide"),
        P("narrow", None, None),
        P(),
        P("narrow", "wide"),
        P(),
        P(),
        P("narrow", "wide"),
        P(),
    )
    out_specs = P("narrow", "wide", None)
    return jax.shard_map(
        per_device, mesh=mesh, in_specs=in_specs, out_specs=out_specs, check_vma=False
    )
```

time: 509 us -> 170 us (0.33)
  the two profiles are of different devices: /device:TPU:4 before, /device:TPU:77 now
where the time goes in v2:
time: 170 us; the launch traced here: 169 us
  waiting for transfers between devices  99.9 us (59%)
  Pallas kernels  28.5 us (17%)
  starting transfers between devices  25.5 us (15%)
  local copies, waits for them, and re-layouts  12.4 us (7%)
  other arithmetic  2.77 us (2%)
    all_to_all x2, waiting for transfers between devices, per_device(): amps.append(lax.all_to_all(block, 'wide', split_axis=0, concat_axis=0))  73.1 us
    pallas_call x2, Pallas kernels, update_rows(): pl.pallas_call(functools.partial(cycle_kernel, start=start, slots=slots,...  28.5 us
    ppermute x13, waiting for transfers between devices, send(): return lax.ppermute(value, AXES, shift(wide * narrow, **way))  26.8 us
    all_to_all x2, starting transfers between devices, per_device(): amps.append(lax.all_to_all(block, 'wide', split_axis=0, concat_axis=0))  18.3 us
    slice x2, local copies, waits for them, and re-layouts, per_device(): block = by_target[:, start:start + rows]  9.29 us
    ppermute x13, starting transfers between devices, send(): return lax.ppermute(value, AXES, shift(wide * narrow, **way))  7.13 us
  transfers between devices with their start and end apart: 15, of which 8 were waited for; matrix products, arithmetic and copies ran while one was open for 9% of the time, Pallas kernels for 10%

profile of v2, /device:TPU:77, one launch (start us, length us, event | category | flops | bytes accessed | tf_op | source)
XLA Modules:
  0.0 169.3 jit_solution(11293454842890460670)
XLA Ops:
  0.0 0.7 collective-permute-start.2
  0.7 1.3 dynamic-slice_bitcast_fusion
  1.9 0.3 collective-permute-start.1
  2.3 1.2 collective-permute-start
  3.5 5.4 %slice.41 = bf16[32,640,128]{2,1,0:T(8,128)(2,1)} slice(bf16[32,1024,128]{2,1,0:T(8,128)(2,1)} %bitcast.26), slice={[0:32], [0:640], [0:128]} | slice | bytes 10485760 | tf_op jit(solution)/shard_map/slice | solution.py:175
  8.9 6.7 %collective-permute-done.1.refs_3_ = bf16[512,512]{1,0:T(8,128)(2,1)S(1)} collective-permute-done((bf16[512,512]{1,0:T(8,128)(2,1)S(1)}, bf16[512,512]{1,0:T(8,128)(2,1)S(1)}, u32[]{:S(2)}, u32[]{:S(2)}) %collective-permute-start.1) | collective-permute-done | bytes 524320 | tf_op jit(solution)/shard_map/ppermute | solution.py:156
  15.6 0.0 copy-start.2
  15.6 0.0 collective-permute-done.refs_2_
  15.6 0.0 copy-start.3
  15.6 0.0 collective-permute-done.2.refs_1_
  15.6 10.4 %all-to-all-start = ((bf16[32,640,128]{2,1,0:T(8,128)(2,1)}), bf16[32,640,128]{2,1,0:T(8,128)(2,1)}, u32[]{:S(2)}, u32[]{:S(2)}) async-start(bf16[32,640,128]{2,1,0:T(8,128)(2,1)} %slice.41), calls=%async_computation | async-start | bytes 10485760 | tf_op jit(solution)/shard_map/all_to_all | solution.py:178
  26.1 1.2 pad_maximum_fusion
  27.3 0.9 collective-permute-start.3
  28.3 0.5 collective-permute-start.4
  28.8 0.0 copy-done.3
  28.8 0.0 copy-done.2
  28.8 1.3 pad_maximum_fusion.2
  30.1 1.2 collective-permute-start.5
  31.3 0.3 collective-permute-start.6
  31.6 3.9 %slice.40 = bf16[32,384,128]{2,1,0:T(8,128)(2,1)} slice(bf16[32,1024,128]{2,1,0:T(8,128)(2,1)} %bitcast.27), slice={[0:32], [640:1024], [0:128]} | slice | bytes 6291456 | tf_op jit(solution)/shard_map/slice | solution.py:175
  35.5 0.0 copy-start.5
  35.5 0.0 copy-start.4
  35.5 0.0 copy-start.10
  35.5 0.0 copy-start.6
  35.5 0.0 copy-start.7
  35.5 61.2 %all-to-all-done.amp_ref = bf16[32,640,128]{2,1,0:T(8,128)(2,1)} async-done(((bf16[32,640,128]{2,1,0:T(8,128)(2,1)}), bf16[32,640,128]{2,1,0:T(8,128)(2,1)}, u32[]{:S(2)}, u32[]{:S(2)}) %all-to-all-start) | async-done | bytes 5242912 | tf_op jit(solution)/shard_map/all_to_all | solution.py:178
  96.8 7.9 %all-to-all-start.1 = ((bf16[32,384,128]{2,1,0:T(8,128)(2,1)}), bf16[32,384,128]{2,1,0:T(8,128)(2,1)S(1)}, u32[]{:S(2)}, u32[]{:S(2)}) async-start(bf16[32,384,128]{2,1,0:T(8,128)(2,1)} %slice.40), calls=%async_computation.1 | async-start | bytes 6291456 | tf_op jit(solution)/shard_map/all_to_all | solution.py:178
  104.6 0.0 collective-permute-done.3.refs_4_
  104.6 0.0 collective-permute-done.4.refs_5_
  104.7 14.9 %collective-permute-done.5.refs_6_ = bf16[768,512]{1,0:T(8,128)(2,1)} collective-permute-done((bf16[768,512]{1,0:T(8,128)(2,1)}, bf16[768,512]{1,0:T(8,128)(2,1)}, u32[]{:S(2)}, u32[]{:S(2)}) %collective-permute-start.5) | collective-permute-done | bytes 786464 | tf_op jit(solution)/shard_map/ppermute | solution.py:156
  119.6 0.0 collective-permute-done.6.refs_7_
  119.6 0.7 collective-permute-start.10
  120.3 0.0 collective-permute-start.9
  120.3 2.1 %collective-permute-done.10.refs_11_ = bf16[768,512]{1,0:T(8,128)(2,1)S(1)} collective-permute-done((bf16[768,512]{1,0:T(8,128)(2,1)}, bf16[768,512]{1,0:T(8,128)(2,1)S(1)}, u32[]{:S(2)}, u32[]{:S(2)}) %collective-permute-start.10) | collective-permute-done | bytes 786464 | tf_op jit(solution)/shard_map/ppermute | solution.py:156
  122.4 0.0 copy-start.8
  122.4 1.1 collective-permute-done.9.refs_10_
  123.6 0.0 copy-start.9
  123.6 0.4 collective-permute-start.11
  123.9 0.1 collective-permute-start.12
  124.1 0.4 collective-permute-start.7
  124.5 0.0 copy-done.8
  124.5 0.0 copy-done.9
  124.5 0.4 collective-permute-start.8
  124.8 0.0 copy-done.5
  124.9 0.0 copy-done.4
  124.9 0.1 reshape.10
  124.9 0.9 copy.12.row_energy_ref
  125.8 0.1 copy.13.row_energy_ref
  126.0 0.1 pad_add_fusion
  126.1 0.0 copy-done.10
  126.1 0.2 select_reduce_fusion
  126.3 0.0 copy-done.6
  126.3 0.0 copy-done.7
  126.3 0.6 concatenate.16.scalar_ref
  126.9 0.0 copy-start.1
  126.9 1.2 collective-permute-done.7.refs_8_
  128.1 0.7 collective-permute-done.8.refs_9_
  128.8 0.0 collective-permute-done.11.refs_12_
  128.8 0.0 collective-permute-done.12.refs_13_
  128.8 17.7 %shard_map.82 = (bf16[1024,2048]{1,0:T(8,128)(2,1)}, bf16[4,4096,512]{2,1,0:T(8,128)(2,1)}) custom-call(s32[122]{0:T(128)} %concatenate.16.scalar_ref, bf16[32,640,128]{2,1,0:T(8,128)(2,1)} %all-to-all-done.amp_ref, f32[640,1]{1,0:T(8,128)} %copy.12.row_energy_ref, f32[4,512]{1,0:T(4,128)} %col_energy_ref.3, bf16[4096,512]{1,0:T(8,128)(2,1)} %bitcast.29, ...), custom_call_target="tpu_custom_call" | custom-call | flops 10737418240 | bytes 24641536 | tf_op jit(solution)/shard_map/pallas_call | solution.py:124
  146.6 11.8 %all-to-all-done.1.amp_ref = bf16[32,384,128]{2,1,0:T(8,128)(2,1)S(1)} async-done(((bf16[32,384,128]{2,1,0:T(8,128)(2,1)}), bf16[32,384,128]{2,1,0:T(8,128)(2,1)S(1)}, u32[]{:S(2)}, u32[]{:S(2)}) %all-to-all-start.1) | async-done | bytes 3145760 | tf_op jit(solution)/shard_map/all_to_all | solution.py:178
  158.4 0.0 copy-done
  158.4 0.0 copy-done.1
  158.4 10.7 %shard_map.83 = bf16[1024,2048]{1,0:T(8,128)(2,1)} custom-call(s32[122]{0:T(128)S(1)} %copy-done.1, bf16[32,384,128]{2,1,0:T(8,128)(2,1)S(1)} %all-to-all-done.1.amp_ref, f32[384,1]{1,0:T(8,128)S(1)} %copy.13.row_energy_ref, f32[4,512]{1,0:T(4,128)S(1)} %copy-done, bf16[4,4096,512]{2,1,0:T(8,128)(2,1)} %get-tuple-element.19.refs_0_, ...), custom_call_target="tpu_custom_call", output_to_operand_aliasing={{}: (5, {})} | custom-call | flops 6442450944 | bytes 21495808 | tf_op jit(solution)/shard_map/pallas_call | solution.py:124
  (5 shorter events, 0.1 us)
Async XLA Ops:
  0.0 15.6 %collective-permute-start.2 = (bf16[4096,512]{1,0:T(8,128)(2,1)}, bf16[4096,512]{1,0:T(8,128)(2,1)}, u32[]{:S(2)}, u32[]{:S(2)}) collective-permute-start(bf16[4096,512]{1,0:T(8,128)(2,1)} %bitcast.28), channel_id=1, source_target_pairs={{0,1},{1,0},{2,3},{3,2},{4,5},{5,4},{6,7},{7,6},{8,9},{9,8},{10,11... | collective-permute-start | bytes 12582920 | tf_op jit(solution)/shard_map/ppermute | solution.py:156
  1.9 13.6 %collective-permute-start.1 = (bf16[512,512]{1,0:T(8,128)(2,1)S(1)}, bf16[512,512]{1,0:T(8,128)(2,1)S(1)}, u32[]{:S(2)}, u32[]{:S(2)}) collective-permute-start(bf16[512,512]{1,0:T(8,128)(2,1)S(1)} %get-tuple-element.21), channel_id=1, source_target_pairs={{0,6},{1,7},{2,0},{3,1},{4,2},{5,3},{6,4},{7,5},{8,14},{9,15},{10,... | collective-permute-start | bytes 1572872 | tf_op jit(solution)/shard_map/ppermute | solution.py:156
  2.3 13.3 %collective-permute-start = (bf16[512,512]{1,0:T(8,128)(2,1)S(1)}, bf16[512,512]{1,0:T(8,128)(2,1)S(1)}, u32[]{:S(2)}, u32[]{:S(2)}) collective-permute-start(bf16[512,512]{1,0:T(8,128)(2,1)S(1)} %get-tuple-element.22), channel_id=1, source_target_pairs={{0,2},{1,3},{2,4},{3,5},{4,6},{5,7},{6,0},{7,1},{8,10},{9,11},{10,... | collective-permute-start | bytes 1572872 | tf_op jit(solution)/shard_map/ppermute | solution.py:156
  15.6 13.3 %copy-start.2 = (bf16[512,512]{1,0:T(8,128)(2,1)}, bf16[512,512]{1,0:T(8,128)(2,1)S(1)}, u32[]{:S(2)}) copy-start(bf16[512,512]{1,0:T(8,128)(2,1)S(1)} %collective-permute-done.1.refs_3_) | copy-start | bytes 1572868
  15.6 13.2 %copy-start.3 = (bf16[512,512]{1,0:T(8,128)(2,1)}, bf16[512,512]{1,0:T(8,128)(2,1)S(1)}, u32[]{:S(2)}) copy-start(bf16[512,512]{1,0:T(8,128)(2,1)S(1)} %collective-permute-done.refs_2_) | copy-start | bytes 1572868
  15.6 81.2 %all-to-all-start = ((bf16[32,640,128]{2,1,0:T(8,128)(2,1)}), bf16[32,640,128]{2,1,0:T(8,128)(2,1)}, u32[]{:S(2)}, u32[]{:S(2)}) async-start(bf16[32,640,128]{2,1,0:T(8,128)(2,1)} %slice.41), calls=%async_computation | async-start | bytes 10485760 | tf_op jit(solution)/shard_map/all_to_all | solution.py:178
  27.3 77.3 %collective-permute-start.3 = (bf16[768,512]{1,0:T(8,128)(2,1)}, bf16[768,512]{1,0:T(8,128)(2,1)}, u32[]{:S(2)}, u32[]{:S(2)}) collective-permute-start(bf16[768,512]{1,0:T(8,128)(2,1)} %get-tuple-element.28), channel_id=1, source_target_pairs={{0,32},{1,33},{2,34},{3,35},{4,36},{5,37},{6,38},{7,39},{8,40},{9,... | collective-permute-start | bytes 2359304 | tf_op jit(solution)/shard_map/ppermute | solution.py:156
  28.3 76.4 %collective-permute-start.4 = (bf16[768,512]{1,0:T(8,128)(2,1)}, bf16[768,512]{1,0:T(8,128)(2,1)}, u32[]{:S(2)}, u32[]{:S(2)}) collective-permute-start(bf16[768,512]{1,0:T(8,128)(2,1)} %get-tuple-element.27), channel_id=1, source_target_pairs={{0,96},{1,97},{2,98},{3,99},{4,100},{5,101},{6,102},{7,103},{8,104... | collective-permute-start | bytes 2359304 | tf_op jit(solution)/shard_map/ppermute | solution.py:156
  30.1 89.5 %collective-permute-start.5 = (bf16[768,512]{1,0:T(8,128)(2,1)}, bf16[768,512]{1,0:T(8,128)(2,1)}, u32[]{:S(2)}, u32[]{:S(2)}) collective-permute-start(bf16[768,512]{1,0:T(8,128)(2,1)} %get-tuple-element.24), channel_id=1, source_target_pairs={{0,8},{1,9},{2,10},{3,11},{4,12},{5,13},{6,14},{7,15},{8,16},{9,17... | collective-permute-start | bytes 2359304 | tf_op jit(solution)/shard_map/ppermute | solution.py:156
  31.3 88.3 %collective-permute-start.6 = (bf16[768,512]{1,0:T(8,128)(2,1)}, bf16[768,512]{1,0:T(8,128)(2,1)}, u32[]{:S(2)}, u32[]{:S(2)}) collective-permute-start(bf16[768,512]{1,0:T(8,128)(2,1)} %get-tuple-element.23), channel_id=1, source_target_pairs={{0,24},{1,25},{2,26},{3,27},{4,28},{5,29},{6,30},{7,31},{8,0},{9,1... | collective-permute-start | bytes 2359304 | tf_op jit(solution)/shard_map/ppermute | solution.py:156
  35.5 89.4 %copy-start.5 = (f32[1,1024]{1,0:T(1,128)S(1)}, f32[1,1024]{1,0:T(1,128)}, u32[]{:S(2)}) copy-start(f32[1,1024]{1,0:T(1,128)} %param.14) | copy-start | bytes 12292
  35.5 89.4 %copy-start.4 = (s32[8,8]{1,0:T(8,128)S(1)}, s32[8,8]{1,0:T(8,128)}, u32[]{:S(2)}) copy-start(s32[8,8]{1,0:T(8,128)} %param.13) | copy-start | bytes 772
  35.5 90.6 %copy-start.10 = (s32[4]{0:T(128)S(1)}, s32[4]{0:T(128)}, u32[]{:S(2)}) copy-start(s32[4]{0:T(128)} %param.10) | copy-start | bytes 52
  35.5 90.8 %copy-start.6 = (s32[1,8]{1,0:T(1,128)S(1)}, s32[1,8]{1,0:T(1,128)}, u32[]{:S(2)}) copy-start(s32[1,8]{1,0:T(1,128)} %param.11) | copy-start | bytes 100
  35.5 90.8 %copy-start.7 = (s32[32]{0:T(128)S(1)}, s32[32]{0:T(128)}, u32[]{:S(2)}) copy-start(s32[32]{0:T(128)} %param.12) | copy-start | bytes 388
  96.8 61.6 %all-to-all-start.1 = ((bf16[32,384,128]{2,1,0:T(8,128)(2,1)}), bf16[32,384,128]{2,1,0:T(8,128)(2,1)S(1)}, u32[]{:S(2)}, u32[]{:S(2)}) async-start(bf16[32,384,128]{2,1,0:T(8,128)(2,1)} %slice.40), calls=%async_computation.1 | async-start | bytes 6291456 | tf_op jit(solution)/shard_map/all_to_all | solution.py:178
  119.6 2.9 %collective-permute-start.10 = (bf16[768,512]{1,0:T(8,128)(2,1)}, bf16[768,512]{1,0:T(8,128)(2,1)S(1)}, u32[]{:S(2)}, u32[]{:S(2)}) collective-permute-start(bf16[768,512]{1,0:T(8,128)(2,1)} %collective-permute-done.4.refs_5_), channel_id=1, source_target_pairs={{0,1},{1,0},{2,3},{3,2},{4,5},{5,4},{6,7},{7,6},{8,9},{9,8},{10,11... | collective-permute-start | bytes 2359304 | tf_op jit(solution)/shard_map/ppermute | solution.py:156
  120.3 3.2 %collective-permute-start.9 = (bf16[768,512]{1,0:T(8,128)(2,1)}, bf16[768,512]{1,0:T(8,128)(2,1)S(1)}, u32[]{:S(2)}, u32[]{:S(2)}) collective-permute-start(bf16[768,512]{1,0:T(8,128)(2,1)} %collective-permute-done.3.refs_4_), channel_id=1, source_target_pairs={{0,1},{1,0},{2,3},{3,2},{4,5},{5,4},{6,7},{7,6},{8,9},{9,8},{10,11... | collective-permute-start | bytes 2359304 | tf_op jit(solution)/shard_map/ppermute | solution.py:156
  122.4 2.0 %copy-start.8 = (bf16[768,512]{1,0:T(8,128)(2,1)}, bf16[768,512]{1,0:T(8,128)(2,1)S(1)}, u32[]{:S(2)}) copy-start(bf16[768,512]{1,0:T(8,128)(2,1)S(1)} %collective-permute-done.10.refs_11_) | copy-start | bytes 2359300
  123.6 0.9 copy-start.9
  123.6 5.3 %collective-permute-start.11 = (bf16[768,512]{1,0:T(8,128)(2,1)}, bf16[768,512]{1,0:T(8,128)(2,1)}, u32[]{:S(2)}, u32[]{:S(2)}) collective-permute-start(bf16[768,512]{1,0:T(8,128)(2,1)} %collective-permute-done.5.refs_6_), channel_id=1, source_target_pairs={{0,1},{1,0},{2,3},{3,2},{4,5},{5,4},{6,7},{7,6},{8,9},{9,8},{10,11... | collective-permute-start | bytes 2359304 | tf_op jit(solution)/shard_map/ppermute | solution.py:156
  123.9 4.9 %collective-permute-start.12 = (bf16[768,512]{1,0:T(8,128)(2,1)}, bf16[768,512]{1,0:T(8,128)(2,1)}, u32[]{:S(2)}, u32[]{:S(2)}) collective-permute-start(bf16[768,512]{1,0:T(8,128)(2,1)} %collective-permute-done.6.refs_7_), channel_id=1, source_target_pairs={{0,1},{1,0},{2,3},{3,2},{4,5},{5,4},{6,7},{7,6},{8,9},{9,8},{10,11... | collective-permute-start | bytes 2359304 | tf_op jit(solution)/shard_map/ppermute | solution.py:156
  124.1 4.0 %collective-permute-start.7 = (bf16[512,512]{1,0:T(8,128)(2,1)}, bf16[512,512]{1,0:T(8,128)(2,1)}, u32[]{:S(2)}, u32[]{:S(2)}) collective-permute-start(bf16[512,512]{1,0:T(8,128)(2,1)} %copy-done.3), channel_id=1, source_target_pairs={{0,1},{1,0},{2,3},{3,2},{4,5},{5,4},{6,7},{7,6},{8,9},{9,8},{10,11... | collective-permute-start | bytes 1572872 | tf_op jit(solution)/shard_map/ppermute | solution.py:156
  124.5 4.4 %collective-permute-start.8 = (bf16[512,512]{1,0:T(8,128)(2,1)}, bf16[512,512]{1,0:T(8,128)(2,1)}, u32[]{:S(2)}, u32[]{:S(2)}) collective-permute-start(bf16[512,512]{1,0:T(8,128)(2,1)} %copy-done.2), channel_id=1, source_target_pairs={{0,1},{1,0},{2,3},{3,2},{4,5},{5,4},{6,7},{7,6},{8,9},{9,8},{10,11... | collective-permute-start | bytes 1572872 | tf_op jit(solution)/shard_map/ppermute | solution.py:156
  126.9 31.5 %copy-start = (f32[4,512]{1,0:T(4,128)S(1)}, f32[4,512]{1,0:T(4,128)}, u32[]{:S(2)}) copy-start(f32[4,512]{1,0:T(4,128)} %col_energy_ref.3) | copy-start | bytes 24580
  126.9 31.5 %copy-start.1 = (s32[122]{0:T(128)S(1)}, s32[122]{0:T(128)}, u32[]{:S(2)}) copy-start(s32[122]{0:T(128)} %concatenate.16.scalar_ref) | copy-start | bytes 1468

commit v3 on v2

--- a/solution.py
+++ b/solution.py
@@ -1,4 +1,5 @@
 import functools
+import math
 import jax
 import jax.numpy as jnp
 from jax import lax
@@ -7,7 +8,7 @@
 from jax.sharding import PartitionSpec as P
 
 AXES = ("wide", "narrow")
-CHUNKS = (640, 384)
+CHUNKS = (704, 320)
 ANY = pl.BlockSpec(memory_space=pl.ANY)
 VMEM = pl.BlockSpec(memory_space=pltpu.VMEM)
 HBM = pl.BlockSpec(memory_space=pltpu.HBM)
@@ -39,6 +40,7 @@
     kept = refs[-1] if cuts else refs[0]
     count = max((which for which, _, _ in cuts), default=-1) + 1
     nbc, rows, blk = amp_ref.shape
+    unit = math.gcd(math.gcd(start, rows), blk)
     qp = staged.shape[2]
     held, slot, row_label = 0, slots, 2 * slots
     col_label = row_label + labels[0]
@@ -63,12 +65,12 @@
         return out
 
     def mask_column(c, carry):
-        for i in range(rows // blk):
-            row = scalar_ref[row_label + start // blk + i]
+        for i in range(rows // unit):
+            row = scalar_ref[row_label + (start + i * unit) // blk]
             kept_block = scalar_ref[table + row * labels[1] + scalar_ref[col_label + c]]
-            tile = amp_ref[c, i * blk:(i + 1) * blk, :]
+            tile = amp_ref[c, i * unit:(i + 1) * unit, :]
             at = pl.multiple_of(c * blk, blk)
-            masked[i * blk:(i + 1) * blk, pl.ds(at, blk)] = tile * kept_block.astype(
+            masked[i * unit:(i + 1) * unit, pl.ds(at, blk)] = tile * kept_block.astype(
                 jnp.float32
             ).astype(tile.dtype)
         return carry

time: 170 us -> 183 us (1.076)
  the two profiles are of different devices: /device:TPU:77 before, /device:TPU:4 now
where the time goes in v3:
time: 183 us; the launch traced here: 182 us
  waiting for transfers between devices  106 us (58%)
  starting transfers between devices  32.7 us (18%)
  Pallas kernels  28.6 us (16%)
  local copies, waits for them, and re-layouts  14 us (8%)
    ppermute x13, waiting for transfers between devices, send(): return lax.ppermute(value, AXES, shift(wide * narrow, **way))  93.7 us
    pallas_call x2, Pallas kernels, update_rows(): pl.pallas_call(functools.partial(cycle_kernel, start=start, slots=slots,...  28.6 us
    all_to_all x2, starting transfers between devices, per_device(): amps.append(lax.all_to_all(block, 'wide', split_axis=0, concat_axis=0))  22.8 us
    all_to_all x2, waiting for transfers between devices, per_device(): amps.append(lax.all_to_all(block, 'wide', split_axis=0, concat_axis=0))  12.6 us
    ppermute x13, starting transfers between devices, send(): return lax.ppermute(value, AXES, shift(wide * narrow, **way))  9.84 us
    slice x2, local copies, waits for them, and re-layouts, per_device(): block = by_target[:, start:start + rows]  8.97 us
  transfers between devices with their start and end apart: 15, of which 7 were waited for; matrix products, arithmetic and copies ran while one was open for 7% of the time, Pallas kernels for 10%

profile of v3, /device:TPU:4, one launch (start us, length us, event | category | flops | bytes accessed | tf_op | source)
XLA Modules:
  0.0 182.4 jit_solution(3031016622215008963)
XLA Ops:
  0.0 0.0 collective-permute-start.2
  0.0 1.3 dynamic-slice_bitcast_fusion
  1.3 0.6 collective-permute-start.1
  1.9 1.5 collective-permute-start
  3.4 5.5 %slice.41 = bf16[32,704,128]{2,1,0:T(8,128)(2,1)} slice(bf16[32,1024,128]{2,1,0:T(8,128)(2,1)} %bitcast.26), slice={[0:32], [0:704], [0:128]} | slice | bytes 11534336 | tf_op jit(solution)/shard_map/slice | solution.py:177
  8.9 6.8 %collective-permute-done.1.refs_3_ = bf16[512,512]{1,0:T(8,128)(2,1)S(1)} collective-permute-done((bf16[512,512]{1,0:T(8,128)(2,1)S(1)}, bf16[512,512]{1,0:T(8,128)(2,1)S(1)}, u32[]{:S(2)}, u32[]{:S(2)}) %collective-permute-start.1) | collective-permute-done | bytes 524320 | tf_op jit(solution)/shard_map/ppermute | solution.py:158
  15.7 0.0 copy-start.2
  15.7 0.3 collective-permute-done.refs_2_
  15.9 0.0 copy-start.3
  15.9 0.0 collective-permute-done.2.refs_1_
  15.9 12.1 %all-to-all-start = ((bf16[32,704,128]{2,1,0:T(8,128)(2,1)}), bf16[32,704,128]{2,1,0:T(8,128)(2,1)}, u32[]{:S(2)}, u32[]{:S(2)}) async-start(bf16[32,704,128]{2,1,0:T(8,128)(2,1)} %slice.41), calls=%async_computation | async-start | bytes 11534336 | tf_op jit(solution)/shard_map/all_to_all | solution.py:180
  28.1 0.1 pad_maximum_fusion
  28.2 1.5 collective-permute-start.3
  29.7 1.8 collective-permute-start.4
  31.5 0.0 copy-done.3
  31.5 0.1 pad_maximum_fusion.2
  31.7 1.5 collective-permute-start.5
  33.2 1.8 collective-permute-start.6
  35.0 74.4 %collective-permute-done.3.refs_4_ = bf16[768,512]{1,0:T(8,128)(2,1)} collective-permute-done((bf16[768,512]{1,0:T(8,128)(2,1)S(1)}, bf16[768,512]{1,0:T(8,128)(2,1)}, u32[]{:S(2)}, u32[]{:S(2)}) %collective-permute-start.3) | collective-permute-done | bytes 786464 | tf_op jit(solution)/shard_map/ppermute | solution.py:158
  109.4 0.2 collective-permute-done.4.refs_5_
  109.6 10.0 %collective-permute-done.5.refs_6_ = bf16[768,512]{1,0:T(8,128)(2,1)S(1)} collective-permute-done((bf16[768,512]{1,0:T(8,128)(2,1)S(1)}, bf16[768,512]{1,0:T(8,128)(2,1)S(1)}, u32[]{:S(2)}, u32[]{:S(2)}) %collective-permute-start.5) | collective-permute-done | bytes 786464 | tf_op jit(solution)/shard_map/ppermute | solution.py:158
  119.6 0.0 copy-start.8
  119.6 0.0 collective-permute-done.6.refs_7_
  119.6 0.9 copy-done.8
  120.5 0.0 copy-start.9
  120.5 0.0 collective-permute-start.10
  120.5 0.9 copy-done.9
  121.4 0.0 collective-permute-start.9
  121.4 3.4 %slice.40 = bf16[32,320,128]{2,1,0:T(8,128)(2,1)} slice(bf16[32,1024,128]{2,1,0:T(8,128)(2,1)} %bitcast.27), slice={[0:32], [704:1024], [0:128]} | slice | bytes 5242880 | tf_op jit(solution)/shard_map/slice | solution.py:177
  124.8 0.0 copy-start.4
  124.9 0.0 copy-start.5
  124.9 0.0 copy-start.10
  124.9 0.0 copy-start.6
  124.9 0.0 copy-start.7
  124.9 0.0 all-to-all-done.amp_ref
  124.9 10.8 %all-to-all-start.1 = ((bf16[32,320,128]{2,1,0:T(8,128)(2,1)}), bf16[32,320,128]{2,1,0:T(8,128)(2,1)S(1)}, u32[]{:S(2)}, u32[]{:S(2)}) async-start(bf16[32,320,128]{2,1,0:T(8,128)(2,1)} %slice.40), calls=%async_computation.1 | async-start | bytes 5242880 | tf_op jit(solution)/shard_map/all_to_all | solution.py:180
  135.6 0.0 collective-permute-done.10.refs_11_
  135.7 0.0 collective-permute-done.9.refs_10_
  135.7 0.1 collective-permute-start.11
  135.8 0.5 collective-permute-start.12
  136.3 0.1 collective-permute-start.7
  136.3 0.0 copy-done.2
  136.4 0.4 collective-permute-start.8
  136.8 0.0 copy-done.4
  136.8 0.0 copy-done.5
  136.8 0.1 reshape.10
  136.9 0.9 copy.12.row_energy_ref
  137.8 0.1 slice_bitcast_fusion.1
  137.8 0.1 copy.13.row_energy_ref
  138.0 0.1 pad_add_fusion
  138.1 0.0 copy-done.10
  138.1 0.2 select_reduce_fusion
  138.3 0.0 copy-done.6
  138.3 0.0 copy-done.7
  138.3 0.7 concatenate.16.scalar_ref
  138.9 2.1 %collective-permute-done.7.refs_8_ = bf16[512,512]{1,0:T(8,128)(2,1)} collective-permute-done((bf16[512,512]{1,0:T(8,128)(2,1)}, bf16[512,512]{1,0:T(8,128)(2,1)}, u32[]{:S(2)}, u32[]{:S(2)}) %collective-permute-start.7) | collective-permute-done | bytes 524320 | tf_op jit(solution)/shard_map/ppermute | solution.py:158
  141.0 0.0 collective-permute-done.8.refs_9_
  141.0 0.0 collective-permute-done.11.refs_12_
  141.0 0.0 collective-permute-done.12.refs_13_
  141.0 18.9 %shard_map.82 = (bf16[1024,2048]{1,0:T(8,128)(2,1)}, bf16[4,4096,512]{2,1,0:T(8,128)(2,1)}) custom-call(s32[122]{0:T(128)} %concatenate.16.scalar_ref, bf16[32,704,128]{2,1,0:T(8,128)(2,1)} %all-to-all-done.amp_ref, f32[704,1]{1,0:T(8,128)} %copy.12.row_energy_ref, f32[4,512]{1,0:T(4,128)} %col_energy_ref.3, bf16[4096,512]{1,0:T(8,128)(2,1)} %bitcast.29, ...), custom_call_target="tpu_custom_call" | custom-call | flops 11811160064 | bytes 25427968 | tf_op jit(solution)/shard_map/pallas_call | solution.py:126
  159.9 12.6 %all-to-all-done.1.amp_ref = bf16[32,320,128]{2,1,0:T(8,128)(2,1)S(1)} async-done(((bf16[32,320,128]{2,1,0:T(8,128)(2,1)}), bf16[32,320,128]{2,1,0:T(8,128)(2,1)S(1)}, u32[]{:S(2)}, u32[]{:S(2)}) %all-to-all-start.1) | async-done | bytes 2621472 | tf_op jit(solution)/shard_map/all_to_all | solution.py:180
  172.6 0.0 copy-done
  172.6 0.0 copy-done.1
  172.6 9.6 %shard_map.83 = bf16[1024,2048]{1,0:T(8,128)(2,1)} custom-call(s32[122]{0:T(128)S(1)} %copy-done.1, bf16[32,320,128]{2,1,0:T(8,128)(2,1)S(1)} %all-to-all-done.1.amp_ref, f32[320,1]{1,0:T(8,128)S(1)} %copy.13.row_energy_ref, f32[4,512]{1,0:T(4,128)S(1)} %copy-done, bf16[4,4096,512]{2,1,0:T(8,128)(2,1)} %get-tuple-element.19.refs_0_, ...), custom_call_target="tpu_custom_call", output_to_operand_aliasing={{}: (5, {})} | custom-call | flops 5368709120 | bytes 20709376 | tf_op jit(solution)/shard_map/pallas_call | solution.py:126
  (5 shorter events, 0.1 us)
Async XLA Ops:
  0.0 15.9 %collective-permute-start.2 = (bf16[4096,512]{1,0:T(8,128)(2,1)}, bf16[4096,512]{1,0:T(8,128)(2,1)}, u32[]{:S(2)}, u32[]{:S(2)}) collective-permute-start(bf16[4096,512]{1,0:T(8,128)(2,1)} %bitcast.28), channel_id=1, source_target_pairs={{0,1},{1,0},{2,3},{3,2},{4,5},{5,4},{6,7},{7,6},{8,9},{9,8},{10,11... | collective-permute-start | bytes 12582920 | tf_op jit(solution)/shard_map/ppermute | solution.py:158
  1.3 14.4 %collective-permute-start.1 = (bf16[512,512]{1,0:T(8,128)(2,1)S(1)}, bf16[512,512]{1,0:T(8,128)(2,1)S(1)}, u32[]{:S(2)}, u32[]{:S(2)}) collective-permute-start(bf16[512,512]{1,0:T(8,128)(2,1)S(1)} %get-tuple-element.21), channel_id=1, source_target_pairs={{0,6},{1,7},{2,0},{3,1},{4,2},{5,3},{6,4},{7,5},{8,14},{9,15},{10,... | collective-permute-start | bytes 1572872 | tf_op jit(solution)/shard_map/ppermute | solution.py:158
  1.9 14.1 %collective-permute-start = (bf16[512,512]{1,0:T(8,128)(2,1)S(1)}, bf16[512,512]{1,0:T(8,128)(2,1)S(1)}, u32[]{:S(2)}, u32[]{:S(2)}) collective-permute-start(bf16[512,512]{1,0:T(8,128)(2,1)S(1)} %get-tuple-element.22), channel_id=1, source_target_pairs={{0,2},{1,3},{2,4},{3,5},{4,6},{5,7},{6,0},{7,1},{8,10},{9,11},{10,... | collective-permute-start | bytes 1572872 | tf_op jit(solution)/shard_map/ppermute | solution.py:158
  15.7 120.7 %copy-start.2 = (bf16[512,512]{1,0:T(8,128)(2,1)}, bf16[512,512]{1,0:T(8,128)(2,1)S(1)}, u32[]{:S(2)}) copy-start(bf16[512,512]{1,0:T(8,128)(2,1)S(1)} %collective-permute-done.1.refs_3_) | copy-start | bytes 1572868
  15.9 15.6 %copy-start.3 = (bf16[512,512]{1,0:T(8,128)(2,1)}, bf16[512,512]{1,0:T(8,128)(2,1)S(1)}, u32[]{:S(2)}) copy-start(bf16[512,512]{1,0:T(8,128)(2,1)S(1)} %collective-permute-done.refs_2_) | copy-start | bytes 1572868
  15.9 108.9 %all-to-all-start = ((bf16[32,704,128]{2,1,0:T(8,128)(2,1)}), bf16[32,704,128]{2,1,0:T(8,128)(2,1)}, u32[]{:S(2)}, u32[]{:S(2)}) async-start(bf16[32,704,128]{2,1,0:T(8,128)(2,1)} %slice.41), calls=%async_computation | async-start | bytes 11534336 | tf_op jit(solution)/shard_map/all_to_all | solution.py:180
  28.2 81.2 %collective-permute-start.3 = (bf16[768,512]{1,0:T(8,128)(2,1)S(1)}, bf16[768,512]{1,0:T(8,128)(2,1)}, u32[]{:S(2)}, u32[]{:S(2)}) collective-permute-start(bf16[768,512]{1,0:T(8,128)(2,1)S(1)} %get-tuple-element.28), channel_id=1, source_target_pairs={{0,32},{1,33},{2,34},{3,35},{4,36},{5,37},{6,38},{7,39},{8,40},{9,... | collective-permute-start | bytes 2359304 | tf_op jit(solution)/shard_map/ppermute | solution.py:158
  29.7 79.9 %collective-permute-start.4 = (bf16[768,512]{1,0:T(8,128)(2,1)S(1)}, bf16[768,512]{1,0:T(8,128)(2,1)}, u32[]{:S(2)}, u32[]{:S(2)}) collective-permute-start(bf16[768,512]{1,0:T(8,128)(2,1)S(1)} %get-tuple-element.27), channel_id=1, source_target_pairs={{0,96},{1,97},{2,98},{3,99},{4,100},{5,101},{6,102},{7,103},{8,104... | collective-permute-start | bytes 2359304 | tf_op jit(solution)/shard_map/ppermute | solution.py:158
  31.7 88.0 %collective-permute-start.5 = (bf16[768,512]{1,0:T(8,128)(2,1)S(1)}, bf16[768,512]{1,0:T(8,128)(2,1)S(1)}, u32[]{:S(2)}, u32[]{:S(2)}) collective-permute-start(bf16[768,512]{1,0:T(8,128)(2,1)S(1)} %get-tuple-element.24), channel_id=1, source_target_pairs={{0,8},{1,9},{2,10},{3,11},{4,12},{5,13},{6,14},{7,15},{8,16},{9,17... | collective-permute-start | bytes 2359304 | tf_op jit(solution)/shard_map/ppermute | solution.py:158
  33.2 86.4 %collective-permute-start.6 = (bf16[768,512]{1,0:T(8,128)(2,1)S(1)}, bf16[768,512]{1,0:T(8,128)(2,1)S(1)}, u32[]{:S(2)}, u32[]{:S(2)}) collective-permute-start(bf16[768,512]{1,0:T(8,128)(2,1)S(1)} %get-tuple-element.23), channel_id=1, source_target_pairs={{0,24},{1,25},{2,26},{3,27},{4,28},{5,29},{6,30},{7,31},{8,0},{9,1... | collective-permute-start | bytes 2359304 | tf_op jit(solution)/shard_map/ppermute | solution.py:158
  119.6 0.9 copy-start.8
  120.5 0.9 copy-start.9
  120.5 15.1 %collective-permute-start.10 = (bf16[768,512]{1,0:T(8,128)(2,1)}, bf16[768,512]{1,0:T(8,128)(2,1)}, u32[]{:S(2)}, u32[]{:S(2)}) collective-permute-start(bf16[768,512]{1,0:T(8,128)(2,1)} %collective-permute-done.4.refs_5_), channel_id=1, source_target_pairs={{0,1},{1,0},{2,3},{3,2},{4,5},{5,4},{6,7},{7,6},{8,9},{9,8},{10,11... | collective-permute-start | bytes 2359304 | tf_op jit(solution)/shard_map/ppermute | solution.py:158
  121.4 14.3 %collective-permute-start.9 = (bf16[768,512]{1,0:T(8,128)(2,1)}, bf16[768,512]{1,0:T(8,128)(2,1)}, u32[]{:S(2)}, u32[]{:S(2)}) collective-permute-start(bf16[768,512]{1,0:T(8,128)(2,1)} %collective-permute-done.3.refs_4_), channel_id=1, source_target_pairs={{0,1},{1,0},{2,3},{3,2},{4,5},{5,4},{6,7},{7,6},{8,9},{9,8},{10,11... | collective-permute-start | bytes 2359304 | tf_op jit(solution)/shard_map/ppermute | solution.py:158
  124.8 11.9 %copy-start.4 = (f32[1,1024]{1,0:T(1,128)S(1)}, f32[1,1024]{1,0:T(1,128)}, u32[]{:S(2)}) copy-start(f32[1,1024]{1,0:T(1,128)} %param.14) | copy-start | bytes 12292
  124.9 11.9 %copy-start.5 = (s32[8,8]{1,0:T(8,128)S(1)}, s32[8,8]{1,0:T(8,128)}, u32[]{:S(2)}) copy-start(s32[8,8]{1,0:T(8,128)} %param.13) | copy-start | bytes 772
  124.9 13.2 %copy-start.10 = (s32[4]{0:T(128)S(1)}, s32[4]{0:T(128)}, u32[]{:S(2)}) copy-start(s32[4]{0:T(128)} %param.10) | copy-start | bytes 52
  124.9 13.4 %copy-start.6 = (s32[1,8]{1,0:T(1,128)S(1)}, s32[1,8]{1,0:T(1,128)}, u32[]{:S(2)}) copy-start(s32[1,8]{1,0:T(1,128)} %param.11) | copy-start | bytes 100
  124.9 13.4 %copy-start.7 = (s32[32]{0:T(128)S(1)}, s32[32]{0:T(128)}, u32[]{:S(2)}) copy-start(s32[32]{0:T(128)} %param.12) | copy-start | bytes 388
  124.9 47.7 %all-to-all-start.1 = ((bf16[32,320,128]{2,1,0:T(8,128)(2,1)}), bf16[32,320,128]{2,1,0:T(8,128)(2,1)S(1)}, u32[]{:S(2)}, u32[]{:S(2)}) async-start(bf16[32,320,128]{2,1,0:T(8,128)(2,1)} %slice.40), calls=%async_computation.1 | async-start | bytes 5242880 | tf_op jit(solution)/shard_map/all_to_all | solution.py:180
  135.7 5.3 %collective-permute-start.11 = (bf16[768,512]{1,0:T(8,128)(2,1)}, bf16[768,512]{1,0:T(8,128)(2,1)}, u32[]{:S(2)}, u32[]{:S(2)}) collective-permute-start(bf16[768,512]{1,0:T(8,128)(2,1)} %copy-done.8), channel_id=1, source_target_pairs={{0,1},{1,0},{2,3},{3,2},{4,5},{5,4},{6,7},{7,6},{8,9},{9,8},{10,11... | collective-permute-start | bytes 2359304 | tf_op jit(solution)/shard_map/ppermute | solution.py:158
  135.8 5.2 %collective-permute-start.12 = (bf16[768,512]{1,0:T(8,128)(2,1)}, bf16[768,512]{1,0:T(8,128)(2,1)}, u32[]{:S(2)}, u32[]{:S(2)}) collective-permute-start(bf16[768,512]{1,0:T(8,128)(2,1)} %copy-done.9), channel_id=1, source_target_pairs={{0,1},{1,0},{2,3},{3,2},{4,5},{5,4},{6,7},{7,6},{8,9},{9,8},{10,11... | collective-permute-start | bytes 2359304 | tf_op jit(solution)/shard_map/ppermute | solution.py:158
  136.3 4.7 %collective-permute-start.7 = (bf16[512,512]{1,0:T(8,128)(2,1)}, bf16[512,512]{1,0:T(8,128)(2,1)}, u32[]{:S(2)}, u32[]{:S(2)}) collective-permute-start(bf16[512,512]{1,0:T(8,128)(2,1)} %copy-done.3), channel_id=1, source_target_pairs={{0,1},{1,0},{2,3},{3,2},{4,5},{5,4},{6,7},{7,6},{8,9},{9,8},{10,11... | collective-permute-start | bytes 1572872 | tf_op jit(solution)/shard_map/ppermute | solution.py:158
  136.4 4.6 %collective-permute-start.8 = (bf16[512,512]{1,0:T(8,128)(2,1)S(1)}, bf16[512,512]{1,0:T(8,128)(2,1)}, u32[]{:S(2)}, u32[]{:S(2)}) collective-permute-start(bf16[512,512]{1,0:T(8,128)(2,1)S(1)} %collective-permute-done.1.refs_3_), channel_id=1, source_target_pairs={{0,1},{1,0},{2,3},{3,2},{4,5},{5,4},{6,7},{7,6},{8,9},{9,8},{10,11... | collective-permute-start | bytes 1572872 | tf_op jit(solution)/shard_map/ppermute | solution.py:158
  138.9 33.6 %copy-start = (f32[4,512]{1,0:T(4,128)S(1)}, f32[4,512]{1,0:T(4,128)}, u32[]{:S(2)}) copy-start(f32[4,512]{1,0:T(4,128)} %col_energy_ref.3) | copy-start | bytes 24580
  138.9 33.6 %copy-start.1 = (s32[122]{0:T(128)S(1)}, s32[122]{0:T(128)}, u32[]{:S(2)}) copy-start(s32[122]{0:T(128)} %concatenate.16.scalar_ref) | copy-start | bytes 1468
